TPU v7x, 32 devices: a whole 2x2x4 slice. The times are simulated.
32 devices in a mesh: gx: 4 (over z), gy: 8 (over y, x, core).
Axes of the slice: x: 2, y: 2, z: 4, core: 2. Of those that a mesh axis runs over, the one named last changes fastest.
Arguments:
- increments: float32 [2, 3, 192, 1024], P(None, None, 'gy', 'gx'), may hold values from -6 to 6
- diffusivity: float32 [3, 192, 1024], P(None, 'gy', 'gx'), may hold values from 0.02 to 0.24
- sea_mask: int32 [192, 1024], P('gy', 'gx'), may hold values 0 or 1
- source_cells: int32 [32, 32, 3, 8, 128], P(('gx', 'gy')), may hold values from 0 to 255, as said below
- source_weights: float32 [32, 32, 8, 128], P(('gx', 'gy')), may hold values from 0.1 to 1
- source_counts: int32 [32, 32, 128], P(('gx', 'gy')), may hold values from 0 to 8
- slot_owner: int32 [32, 32, 128], P(('gx', 'gy')), may hold values from 0 to 4095
Outputs:
- smoothed: float32 [2, 3, 192, 1024], P(None, None, 'gy', 'gx')
- obs_equiv: float32 [131072], P(('gx', 'gy'))
Inputs may be any that keep to these rules, and one draw needn't show every extreme that they name: `source_cells`: component 0 is a layer below 6, component 1 a row below 24, component 2 a column below 256, all within the grid device's own tile. `source_counts`: number of leading valid entries of the slot; 0 leaves the slot empty. `slot_owner`: an observation index local to the owner.
All inputs are finite; a program needn't handle non-finite values. No bound on the sum of `sea_mask` on one device may be relied on, other than what follows from the above.
Results may differ from a plain program's by a relative error of at most 0.00002.
Values sent between devices are 32-bit elements; how exact they have to be, the bound alone decides.
A program may use at most 64 MiB of HBM per device.

v0:
```python
import jax
import jax.numpy as jnp
from jax import lax
from jax.sharding import PartitionSpec as P

ITERS = 10
OBS_DEV = 4096


def padded(shard, sides, width):
    for axis, dim in sides:
        size, length = (lax.axis_size(axis), shard.shape[dim])
        up = [(i, (i + 1) % size) for i in range(size)]
        down = [(j, i) for i, j in up]
        last = lax.slice_in_dim(shard, length - width, length, axis=dim)
        first = lax.slice_in_dim(shard, 0, width, axis=dim)
        before = lax.ppermute(last, axis, up)
        after = lax.ppermute(first, axis, down)
        shard = jnp.concatenate([before, shard, after], axis=dim)
    return shard


def column_widen(array):
    wider = padded(array, ((("gx", "gy"), 1),), 1)
    return jnp.pad(wider, ((0, 0), (0, 0), (1, 1)))


def coefficient_set(diffuse_wide, wet_wide):
    centre_k = diffuse_wide[:, 1:-1, 1:-1]
    centre_w = wet_wide[1:-1, 1:-1]
    up_first = 0.5 * (centre_k + diffuse_wide[:, 2:, 1:-1]) * centre_w * wet_wide[2:, 1:-1]
    down_first = 0.5 * (centre_k + diffuse_wide[:, :-2, 1:-1]) * centre_w * wet_wide[:-2, 1:-1]
    up_second = 0.5 * (centre_k + diffuse_wide[:, 1:-1, 2:]) * centre_w * wet_wide[1:-1, 2:]
    down_second = 0.5 * (centre_k + diffuse_wide[:, 1:-1, :-2]) * centre_w * wet_wide[1:-1, :-2]
    return (up_first, down_first, up_second, down_second)


def relax(wide, coeffs, nfields, nlevels):
    span_a = wide.shape[1] - 2
    span_b = wide.shape[2] - 2
    grid = wide.reshape(nfields, nlevels, span_a + 2, span_b + 2)
    up_first, down_first, up_second, down_second = coeffs
    centre = grid[:, :, 1:-1, 1:-1]
    first_part = up_first * (grid[:, :, 2:, 1:-1] - centre) - down_first * (
        centre - grid[:, :, :-2, 1:-1]
    )
    second_part = up_second * (grid[:, :, 1:-1, 2:] - centre) - down_second * (
        centre - grid[:, :, 1:-1, :-2]
    )
    updated = centre + second_part + first_part
    return updated.reshape(nfields * nlevels, span_a, span_b)


def local(
    increments, diffusivity, sea_mask, source_cells, source_weights, source_counts, slot_owner
):
    nfields, nlevels, tile_rows, tile_cols = increments.shape
    layers = nfields * nlevels
    wet = sea_mask.astype(jnp.float32)
    started = (increments * wet).reshape(layers, tile_rows, tile_cols)
    stacked = jnp.concatenate([started, diffusivity, wet[None]], axis=0)
    moved = lax.all_to_all(stacked, "gy", split_axis=2, concat_axis=1, tiled=True)
    moved = jnp.transpose(moved, (0, 2, 1))
    field = moved[:layers]
    outer = column_widen(moved[layers:])
    coeffs = coefficient_set(outer[:nlevels], outer[nlevels])

    def advance(turn_index, flat_field):
        return relax(column_widen(flat_field), coeffs, nfields, nlevels)

    field = lax.fori_loop(0, ITERS, advance, field)
    field = lax.all_to_all(
        jnp.transpose(field, (0, 2, 1)), "gy", split_axis=1, concat_axis=2, tiled=True
    )
    smoothed = field.reshape(nfields, nlevels, tile_rows, tile_cols)
    flat_tile = smoothed.reshape(-1)
    cells_here = source_cells[0]
    flat_index = (cells_here[:, 0] * tile_rows + cells_here[:, 1]) * tile_cols + cells_here[:, 2]
    values = flat_tile[flat_index]
    valid = lax.broadcasted_iota(jnp.int32, flat_index.shape, 1) < source_counts[0][:, None, :]
    partial_value = jnp.sum(jnp.where(valid, source_weights[0] * values, jnp.float32(0.0)), axis=1)
    received = lax.all_to_all(partial_value, ("gx", "gy"), split_axis=0, concat_axis=0, tiled=True)
    obs_equiv = (
        jnp.zeros((OBS_DEV,), jnp.float32).at[slot_owner[0].reshape(-1)].add(received.reshape(-1))
    )
    return (smoothed, obs_equiv)


def solution(mesh):
    return jax.shard_map(
        local,
        mesh=mesh,
        in_specs=(
            P(None, None, "gy", "gx"),
            P(None, "gy", "gx"),
            P("gy", "gx"),
            P(("gx", "gy"), None, None, None, None),
            P(("gx", "gy"), None, None, None),
            P(("gx", "gy"), None, None),
            P(("gx", "gy"), None, None),
        ),
        out_specs=(P(None, None, "gy", "gx"), P(("gx", "gy"))),
        check_vma=False,
    )
```

profile of v0, /device:TPU:0, one launch (start us, length us, event | category | flops | bytes accessed | tf_op | source)
XLA Modules:
  0.0 331.4 jit_solution(478034982832451577)
XLA Ops:
  1.4 0.9 broadcast_multiply_fusion
  2.3 0.9 pad_maximum_fusion
  3.2 1.3 copy.24
  4.5 0.9 reshape.139
  5.4 11.7 %all_to_all.42 = f32[8,1,7680]{2,1,0:T(1,128)S(1)} all-to-all(f32[8,1,7680]{2,1,0:T(1,128)S(1)} %reshape.139), channel_id=1, replica_groups=mesh['gx'=4,'gy'=8] {'gy'}, dimensions={0} | all-to-all | bytes 491520 | tf_op jit(solution)/shard_map/all_to_all | solution.py:62
  17.8 1.3 reduce
  21.0 5.3 %collective-permute-start.3 = (f32[4,1,192]{2,1,0:T(1,128)S(1)}, f32[4,1,192]{2,1,0:T(1,128)S(1)}, u32[]{:S(2)}, u32[]{:S(2)}) collective-permute-start(f32[4,1,192]{2,1,0:T(1,128)S(1)} %get-tuple-element.101), channel_id=1, source_target_pairs={{1,0},{2,1},{3,2},{4,3},{5,4},{6,5},{7,6},{8,7},{9,8},{10,9},{11,1... | collective-permute-start | bytes 9224 | tf_op jit(solution)/shard_map/ppermute | solution.py:18
  26.4 1.3 collective-permute-done.2
  28.0 77.7 %while.12 = (s32[]{:T(128)}, f32[6,32,192]{2,1,0:T(8,128)S(1)}, f32[3,32,192]{2,1,0:T(8,128)S(1)}, f32[3,32,192]{2,1,0:T(8,128)S(1)}, f32[3,32,192]{2,1,0:T(8,128)S(1)}, /*index=5*/f32[3,32,192]{2,1,0:T(8,128)S(1)}, s32[]{:T(128)}) while((s32[]{:T(128)}, f32[6,32,192]{2,1,0:T(8,128)S(1)}, f32[3,32,192]{2,1,0:T(8,128)S(1)}, ...), condition=%wide.region_1.2_spmd, body=%wide.region_0.1_spmd.sunk | while | flops 758978 | bytes 1550077 | solution.py:71
  28.1 5.4 %collective-permute-start = (f32[6,1,192]{2,1,0:T(1,128)S(1)}, f32[6,1,192]{2,1,0:T(1,128)S(1)}, u32[]{:S(2)}, u32[]{:S(2)}) collective-permute-start(f32[6,1,192]{2,1,0:T(1,128)S(1)} %get-tuple-element.148), channel_id=1, source_target_pairs={{1,0},{2,1},{3,2},{4,3},{5,4},{6,5},{7,6},{8,7},{9,8},{10,9},{11,1... | collective-permute-start | bytes 13832 | tf_op jit(solution)/shard_map/while/body/eval_jaxpr/ppermute | solution.py:18
  33.4 1.3 collective-permute-done
  34.8 5.3 %collective-permute-done.1 = f32[6,1,192]{2,1,0:T(1,128)S(1)} collective-permute-done((f32[6,1,192]{2,1,0:T(1,128)S(1)}, f32[6,1,192]{2,1,0:T(1,128)S(1)}, u32[]{:S(2)}, u32[]{:S(2)}) %collective-permute-start.1) | collective-permute-done | bytes 4640 | tf_op jit(solution)/shard_map/while/body/eval_jaxpr/ppermute | solution.py:17
  42.0 5.4 %collective-permute-done.1 = f32[6,1,192]{2,1,0:T(1,128)S(1)} collective-permute-done((f32[6,1,192]{2,1,0:T(1,128)S(1)}, f32[6,1,192]{2,1,0:T(1,128)S(1)}, u32[]{:S(2)}, u32[]{:S(2)}) %collective-permute-start.1) | collective-permute-done | bytes 4640 | tf_op jit(solution)/shard_map/while/body/eval_jaxpr/ppermute | solution.py:17
  49.2 5.4 %collective-permute-done.1 = f32[6,1,192]{2,1,0:T(1,128)S(1)} collective-permute-done((f32[6,1,192]{2,1,0:T(1,128)S(1)}, f32[6,1,192]{2,1,0:T(1,128)S(1)}, u32[]{:S(2)}, u32[]{:S(2)}) %collective-permute-start.1) | collective-permute-done | bytes 4640 | tf_op jit(solution)/shard_map/while/body/eval_jaxpr/ppermute | solution.py:17
  56.5 5.4 %collective-permute-done.1 = f32[6,1,192]{2,1,0:T(1,128)S(1)} collective-permute-done((f32[6,1,192]{2,1,0:T(1,128)S(1)}, f32[6,1,192]{2,1,0:T(1,128)S(1)}, u32[]{:S(2)}, u32[]{:S(2)}) %collective-permute-start.1) | collective-permute-done | bytes 4640 | tf_op jit(solution)/shard_map/while/body/eval_jaxpr/ppermute | solution.py:17
  63.7 5.4 %collective-permute-done.1 = f32[6,1,192]{2,1,0:T(1,128)S(1)} collective-permute-done((f32[6,1,192]{2,1,0:T(1,128)S(1)}, f32[6,1,192]{2,1,0:T(1,128)S(1)}, u32[]{:S(2)}, u32[]{:S(2)}) %collective-permute-start.1) | collective-permute-done | bytes 4640 | tf_op jit(solution)/shard_map/while/body/eval_jaxpr/ppermute | solution.py:17
  71.0 5.4 %collective-permute-done.1 = f32[6,1,192]{2,1,0:T(1,128)S(1)} collective-permute-done((f32[6,1,192]{2,1,0:T(1,128)S(1)}, f32[6,1,192]{2,1,0:T(1,128)S(1)}, u32[]{:S(2)}, u32[]{:S(2)}) %collective-permute-start.1) | collective-permute-done | bytes 4640 | tf_op jit(solution)/shard_map/while/body/eval_jaxpr/ppermute | solution.py:17
  77.4 0.8 collective-permute-done
  78.2 5.4 %collective-permute-done.1 = f32[6,1,192]{2,1,0:T(1,128)S(1)} collective-permute-done((f32[6,1,192]{2,1,0:T(1,128)S(1)}, f32[6,1,192]{2,1,0:T(1,128)S(1)}, u32[]{:S(2)}, u32[]{:S(2)}) %collective-permute-start.1) | collective-permute-done | bytes 4640 | tf_op jit(solution)/shard_map/while/body/eval_jaxpr/ppermute | solution.py:17
  84.6 0.8 collective-permute-done
  85.5 5.4 %collective-permute-done.1 = f32[6,1,192]{2,1,0:T(1,128)S(1)} collective-permute-done((f32[6,1,192]{2,1,0:T(1,128)S(1)}, f32[6,1,192]{2,1,0:T(1,128)S(1)}, u32[]{:S(2)}, u32[]{:S(2)}) %collective-permute-start.1) | collective-permute-done | bytes 4640 | tf_op jit(solution)/shard_map/while/body/eval_jaxpr/ppermute | solution.py:17
  92.7 5.4 %collective-permute-done.1 = f32[6,1,192]{2,1,0:T(1,128)S(1)} collective-permute-done((f32[6,1,192]{2,1,0:T(1,128)S(1)}, f32[6,1,192]{2,1,0:T(1,128)S(1)}, u32[]{:S(2)}, u32[]{:S(2)}) %collective-permute-start.1) | collective-permute-done | bytes 4640 | tf_op jit(solution)/shard_map/while/body/eval_jaxpr/ppermute | solution.py:17
  100.0 5.4 %collective-permute-done.1 = f32[6,1,192]{2,1,0:T(1,128)S(1)} collective-permute-done((f32[6,1,192]{2,1,0:T(1,128)S(1)}, f32[6,1,192]{2,1,0:T(1,128)S(1)}, u32[]{:S(2)}, u32[]{:S(2)}) %collective-permute-start.1) | collective-permute-done | bytes 4640 | tf_op jit(solution)/shard_map/while/body/eval_jaxpr/ppermute | solution.py:17
  106.2 1.0 reshape.141
  107.2 3.4 %all-to-all-start.1 = ((f32[8,1,4608]{2,1,0:T(1,128)}), f32[8,1,4608]{2,1,0:T(1,128)S(1)}, u32[]{:S(2)}, u32[]{:S(2)}) async-start(f32[8,1,4608]{2,1,0:T(1,128)} %reshape.141), calls=%async_computation.1 | async-start | bytes 294912 | tf_op jit(solution)/shard_map/all_to_all | solution.py:72
  110.6 5.6 %all-to-all-done.1 = f32[8,1,4608]{2,1,0:T(1,128)S(1)} async-done(((f32[8,1,4608]{2,1,0:T(1,128)}), f32[8,1,4608]{2,1,0:T(1,128)S(1)}, u32[]{:S(2)}, u32[]{:S(2)}) %all-to-all-start.1) | async-done | bytes 147488 | tf_op jit(solution)/shard_map/all_to_all | solution.py:72
  116.2 1.0 reduce.1
  118.1 180.5 %gather_fusion = f32[32768]{0:T(1024)S(1)} fusion(f32[36864]{0:T(1024)S(1)} %reshape_reshape.3, s32[32768]{0:T(1024)S(1)} %fusion.11), kind=kCustom, calls=%fused_computation | custom fusion | bytes 393216 | tf_op jit(solution)/shard_map/gather | solution.py:79
  299.3 2.5 all-to-all-start.2
  301.9 0.9 reshape.118
  302.7 6.2 %all-to-all-done.2 = f32[32,1,128]{2,1,0:T(1,128)S(1)} async-done(((f32[32,1,128]{2,1,0:T(1,128)}), f32[32,1,128]{2,1,0:T(1,128)S(1)}, u32[]{:S(2)}, u32[]{:S(2)}) %all-to-all-start.2) | async-done | bytes 16416 | tf_op jit(solution)/shard_map/all_to_all | solution.py:82
  308.9 22.5 %scatter_custom_fusion = f32[4096]{0:T(1024)} fusion(s32[4096]{0:T(1024)S(1)} %bitcast.71, f32[4096]{0:T(1024)S(1)} %bitcast.70, f32[]{:T(128)} %constant.27.clone.1), kind=kCustom, calls=%fused_computation.55 | custom fusion | flops 4096 | bytes 16388 | tf_op jit(solution)/shard_map/scatter-add | solution.py:84
  (86 shorter events, 20.9 us)
Async XLA Ops:
  21.0 6.7 %collective-permute-start.2 = (f32[4,1,192]{2,1,0:T(1,128)S(1)}, f32[4,1,192]{2,1,0:T(1,128)S(1)}, u32[]{:S(2)}, u32[]{:S(2)}) collective-permute-start(f32[4,1,192]{2,1,0:T(1,128)S(1)} %get-tuple-element.100), channel_id=1, source_target_pairs={{0,1},{1,2},{2,3},{3,4},{4,5},{5,6},{6,7},{7,8},{8,9},{9,10},{10,1... | collective-permute-start | bytes 9224 | tf_op jit(solution)/shard_map/ppermute | solution.py:17
  21.0 6.7 %collective-permute-start.3 = (f32[4,1,192]{2,1,0:T(1,128)S(1)}, f32[4,1,192]{2,1,0:T(1,128)S(1)}, u32[]{:S(2)}, u32[]{:S(2)}) collective-permute-start(f32[4,1,192]{2,1,0:T(1,128)S(1)} %get-tuple-element.101), channel_id=1, source_target_pairs={{1,0},{2,1},{3,2},{4,3},{5,4},{6,5},{7,6},{8,7},{9,8},{10,9},{11,1... | collective-permute-start | bytes 9224 | tf_op jit(solution)/shard_map/ppermute | solution.py:18
  28.1 6.7 %collective-permute-start = (f32[6,1,192]{2,1,0:T(1,128)S(1)}, f32[6,1,192]{2,1,0:T(1,128)S(1)}, u32[]{:S(2)}, u32[]{:S(2)}) collective-permute-start(f32[6,1,192]{2,1,0:T(1,128)S(1)} %get-tuple-element.148), channel_id=1, source_target_pairs={{1,0},{2,1},{3,2},{4,3},{5,4},{6,5},{7,6},{8,7},{9,8},{10,9},{11,1... | collective-permute-start | bytes 13832 | tf_op jit(solution)/shard_map/while/body/eval_jaxpr/ppermute | solution.py:18
  33.4 6.7 %collective-permute-start.1 = (f32[6,1,192]{2,1,0:T(1,128)S(1)}, f32[6,1,192]{2,1,0:T(1,128)S(1)}, u32[]{:S(2)}, u32[]{:S(2)}) collective-permute-start(f32[6,1,192]{2,1,0:T(1,128)S(1)} %get-tuple-element.149), channel_id=1, source_target_pairs={{0,1},{1,2},{2,3},{3,4},{4,5},{5,6},{6,7},{7,8},{8,9},{9,10},{10,1... | collective-permute-start | bytes 13832 | tf_op jit(solution)/shard_map/while/body/eval_jaxpr/ppermute | solution.py:17
  40.6 1.4 collective-permute-start
  40.6 6.7 %collective-permute-start.1 = (f32[6,1,192]{2,1,0:T(1,128)S(1)}, f32[6,1,192]{2,1,0:T(1,128)S(1)}, u32[]{:S(2)}, u32[]{:S(2)}) collective-permute-start(f32[6,1,192]{2,1,0:T(1,128)S(1)} %get-tuple-element.149), channel_id=1, source_target_pairs={{0,1},{1,2},{2,3},{3,4},{4,5},{5,6},{6,7},{7,8},{8,9},{9,10},{10,1... | collective-permute-start | bytes 13832 | tf_op jit(solution)/shard_map/while/body/eval_jaxpr/ppermute | solution.py:17
  47.8 1.4 collective-permute-start
  47.9 6.7 %collective-permute-start.1 = (f32[6,1,192]{2,1,0:T(1,128)S(1)}, f32[6,1,192]{2,1,0:T(1,128)S(1)}, u32[]{:S(2)}, u32[]{:S(2)}) collective-permute-start(f32[6,1,192]{2,1,0:T(1,128)S(1)} %get-tuple-element.149), channel_id=1, source_target_pairs={{0,1},{1,2},{2,3},{3,4},{4,5},{5,6},{6,7},{7,8},{8,9},{9,10},{10,1... | collective-permute-start | bytes 13832 | tf_op jit(solution)/shard_map/while/body/eval_jaxpr/ppermute | solution.py:17
  55.1 1.4 collective-permute-start
  55.1 6.7 %collective-permute-start.1 = (f32[6,1,192]{2,1,0:T(1,128)S(1)}, f32[6,1,192]{2,1,0:T(1,128)S(1)}, u32[]{:S(2)}, u32[]{:S(2)}) collective-permute-start(f32[6,1,192]{2,1,0:T(1,128)S(1)} %get-tuple-element.149), channel_id=1, source_target_pairs={{0,1},{1,2},{2,3},{3,4},{4,5},{5,6},{6,7},{7,8},{8,9},{9,10},{10,1... | collective-permute-start | bytes 13832 | tf_op jit(solution)/shard_map/while/body/eval_jaxpr/ppermute | solution.py:17
  62.3 1.4 collective-permute-start
  62.4 6.7 %collective-permute-start.1 = (f32[6,1,192]{2,1,0:T(1,128)S(1)}, f32[6,1,192]{2,1,0:T(1,128)S(1)}, u32[]{:S(2)}, u32[]{:S(2)}) collective-permute-start(f32[6,1,192]{2,1,0:T(1,128)S(1)} %get-tuple-element.149), channel_id=1, source_target_pairs={{0,1},{1,2},{2,3},{3,4},{4,5},{5,6},{6,7},{7,8},{8,9},{9,10},{10,1... | collective-permute-start | bytes 13832 | tf_op jit(solution)/shard_map/while/body/eval_jaxpr/ppermute | solution.py:17
  69.6 1.4 collective-permute-start
  69.6 6.7 %collective-permute-start.1 = (f32[6,1,192]{2,1,0:T(1,128)S(1)}, f32[6,1,192]{2,1,0:T(1,128)S(1)}, u32[]{:S(2)}, u32[]{:S(2)}) collective-permute-start(f32[6,1,192]{2,1,0:T(1,128)S(1)} %get-tuple-element.149), channel_id=1, source_target_pairs={{0,1},{1,2},{2,3},{3,4},{4,5},{5,6},{6,7},{7,8},{8,9},{9,10},{10,1... | collective-permute-start | bytes 13832 | tf_op jit(solution)/shard_map/while/body/eval_jaxpr/ppermute | solution.py:17
  76.8 1.4 collective-permute-start
  76.9 6.7 %collective-permute-start.1 = (f32[6,1,192]{2,1,0:T(1,128)S(1)}, f32[6,1,192]{2,1,0:T(1,128)S(1)}, u32[]{:S(2)}, u32[]{:S(2)}) collective-permute-start(f32[6,1,192]{2,1,0:T(1,128)S(1)} %get-tuple-element.149), channel_id=1, source_target_pairs={{0,1},{1,2},{2,3},{3,4},{4,5},{5,6},{6,7},{7,8},{8,9},{9,10},{10,1... | collective-permute-start | bytes 13832 | tf_op jit(solution)/shard_map/while/body/eval_jaxpr/ppermute | solution.py:17
  84.1 1.4 collective-permute-start
  84.1 6.7 %collective-permute-start.1 = (f32[6,1,192]{2,1,0:T(1,128)S(1)}, f32[6,1,192]{2,1,0:T(1,128)S(1)}, u32[]{:S(2)}, u32[]{:S(2)}) collective-permute-start(f32[6,1,192]{2,1,0:T(1,128)S(1)} %get-tuple-element.149), channel_id=1, source_target_pairs={{0,1},{1,2},{2,3},{3,4},{4,5},{5,6},{6,7},{7,8},{8,9},{9,10},{10,1... | collective-permute-start | bytes 13832 | tf_op jit(solution)/shard_map/while/body/eval_jaxpr/ppermute | solution.py:17
  91.3 1.4 collective-permute-start
  91.4 6.7 %collective-permute-start.1 = (f32[6,1,192]{2,1,0:T(1,128)S(1)}, f32[6,1,192]{2,1,0:T(1,128)S(1)}, u32[]{:S(2)}, u32[]{:S(2)}) collective-permute-start(f32[6,1,192]{2,1,0:T(1,128)S(1)} %get-tuple-element.149), channel_id=1, source_target_pairs={{0,1},{1,2},{2,3},{3,4},{4,5},{5,6},{6,7},{7,8},{8,9},{9,10},{10,1... | collective-permute-start | bytes 13832 | tf_op jit(solution)/shard_map/while/body/eval_jaxpr/ppermute | solution.py:17
  98.5 1.4 collective-permute-start
  98.6 6.7 %collective-permute-start.1 = (f32[6,1,192]{2,1,0:T(1,128)S(1)}, f32[6,1,192]{2,1,0:T(1,128)S(1)}, u32[]{:S(2)}, u32[]{:S(2)}) collective-permute-start(f32[6,1,192]{2,1,0:T(1,128)S(1)} %get-tuple-element.149), channel_id=1, source_target_pairs={{0,1},{1,2},{2,3},{3,4},{4,5},{5,6},{6,7},{7,8},{8,9},{9,10},{10,1... | collective-permute-start | bytes 13832 | tf_op jit(solution)/shard_map/while/body/eval_jaxpr/ppermute | solution.py:17
  105.8 4.8 %copy-start = (s32[1,32,3,8,128]{4,3,2,1,0:T(8,128)S(1)}, s32[1,32,3,8,128]{4,3,2,1,0:T(8,128)}, u32[]{:S(2)}) copy-start(s32[1,32,3,8,128]{4,3,2,1,0:T(8,128)} %param.12) | copy-start | bytes 1179652
  107.2 9.0 %all-to-all-start.1 = ((f32[8,1,4608]{2,1,0:T(1,128)}), f32[8,1,4608]{2,1,0:T(1,128)S(1)}, u32[]{:S(2)}, u32[]{:S(2)}) async-start(f32[8,1,4608]{2,1,0:T(1,128)} %reshape.141), calls=%async_computation.1 | async-start | bytes 294912 | tf_op jit(solution)/shard_map/all_to_all | solution.py:72
  118.0 180.6 %copy-start.1 = (f32[1,32,8,128]{3,2,1,0:T(8,128)S(1)}, f32[1,32,8,128]{3,2,1,0:T(8,128)}, u32[]{:S(2)}) copy-start(f32[1,32,8,128]{3,2,1,0:T(8,128)} %param.13) | copy-start | bytes 393220
  118.1 180.6 %copy-start.2 = (s32[1,32,128]{2,1,0:T(8,128)S(1)}, s32[1,32,128]{2,1,0:T(8,128)}, u32[]{:S(2)}) copy-start(s32[1,32,128]{2,1,0:T(8,128)} %param.14) | copy-start | bytes 49156
  118.1 183.8 %copy-start.3 = (s32[1,32,128]{2,1,0:T(8,128)S(1)}, s32[1,32,128]{2,1,0:T(8,128)}, u32[]{:S(2)}) copy-start(s32[1,32,128]{2,1,0:T(8,128)} %param.15) | copy-start | bytes 49156
  299.3 9.6 %all-to-all-start.2 = ((f32[32,1,128]{2,1,0:T(1,128)}), f32[32,1,128]{2,1,0:T(1,128)S(1)}, u32[]{:S(2)}, u32[]{:S(2)}) async-start(f32[32,1,128]{2,1,0:T(1,128)} %bitcast.22), calls=%async_computation.2 | async-start | bytes 32768 | tf_op jit(solution)/shard_map/all_to_all | solution.py:82
where the time goes:
time: 332 us; the launch traced here: 331 us
  local copies, waits for them, and re-layouts  188 us (57%)
  waiting for transfers between devices  75.5 us (23%)
  other arithmetic  32.7 us (10%)
  starting transfers between devices  21.7 us (7%)
  blocking collectives  11.7 us (4%)
    gather x1, local copies, waits for them, and re-layouts, local(): values = flat_tile[flat_index]  181 us
    ppermute x11, waiting for transfers between devices, padded(): before = lax.ppermute(last, axis, up)  54.8 us
    scatter-add x1, other arithmetic, local(): jnp.zeros((OBS_DEV,), jnp.float32).at[slot_owner[0].reshape(-1)]  22.5 us
    all_to_all x1, blocking collectives, local(): lax.all_to_all(stacked, 'gy', split_axis=2, concat_axis=1, tiled=True)  11.7 us
    ppermute x11, starting transfers between devices, padded(): after = lax.ppermute(first, axis, down)  11.2 us
    ppermute x11, waiting for transfers between devices, padded(): after = lax.ppermute(first, axis, down)  8.97 us
  transfers between devices with their start and end apart: 24, of which 23 were waited for; matrix products, arithmetic and copies ran while one was open for 0% of the time, Pallas kernels for 0%

commit v1 on v0

v1 whole, which is shorter than its diff:
```python
import functools

import jax
import jax.numpy as jnp
from jax import lax
from jax.experimental import pallas as pl
from jax.experimental.pallas import tpu as pltpu
from jax.sharding import PartitionSpec as P

ITERS = 10
OBS_DEV = 4096
LANES = 128
EDGE = 12
MESH = pl.DeviceIdType.MESH
GROUP = 8


def kernel(
    nx, ny, inc, dif, mask, cells, weights, counts, owner, smoothed, obs,
    ext, c_east, c_north, to_prev, to_next, first_cols, last_cols,
    from_prev, from_next, east_mid, east_next, east_prev, west_mid, west_next, west_prev,
    table, part, recv, halo_send, halo_recv, part_send, part_recv,
):
    nfields, nlevels, rows, cols = inc.shape
    layers = nfields * nlevels
    total = layers + nlevels + 1
    high, wide = ext.shape[1:]
    devices = nx * ny
    gx, gy = lax.axis_index("gx"), lax.axis_index("gy")
    me = gx * ny + gy

    def place(step):
        other = lax.rem(me + step, devices)
        return other, (lax.div(other, ny), lax.rem(other, ny))

    barrier = pltpu.get_barrier_semaphore()

    def greet(step, carry):
        pl.semaphore_signal(barrier, inc=1, device_id=place(step)[1], device_id_type=MESH)
        return carry

    lax.fori_loop(1, devices, greet, 0)

    lane = lax.broadcasted_iota(jnp.int32, (rows, LANES), 1)
    wet = mask[...].astype(jnp.float32)
    packed_first = jnp.zeros((rows, LANES), jnp.float32)
    packed_last = jnp.zeros((rows, LANES), jnp.float32)
    for k in range(total):
        if k < layers:
            value = inc[k // nlevels, k % nlevels] * wet
        elif k < layers + nlevels:
            value = dif[k - layers]
        else:
            value = wet
        ext[k, 0:rows, 0:cols] = value
        ext[k, 32:40, 0:cols] = jnp.zeros((8, cols), jnp.float32)
        to_next[ITERS * k : ITERS * (k + 1), :] = value[rows - ITERS : rows]
        to_prev[ITERS * k : ITERS * (k + 1), :] = value[0:ITERS]
        here = (lane >= EDGE * k) & (lane < EDGE * (k + 1))
        first = value[:, 0:LANES]
        last = value[:, cols - LANES : cols]
        if k:
            first = pltpu.roll(first, EDGE * k, 1)
        last = pltpu.roll(last, (EDGE * k + EDGE) % LANES, 1)
        packed_first = jnp.where(here, first, packed_first)
        packed_last = jnp.where(here, last, packed_last)
    first_cols[...] = packed_first
    last_cols[...] = packed_last

    pl.semaphore_wait(barrier, devices - 1)

    east, west = lax.rem(gx + 1, nx), lax.rem(gx + nx - 1, nx)
    north, south = lax.rem(gy + 1, ny), lax.rem(gy + ny - 1, ny)
    plan = [
        (to_next, from_prev, (gx, north)),
        (to_prev, from_next, (gx, south)),
        (first_cols, east_mid, (west, gy)),
        (last_cols, west_mid, (east, gy)),
        (first_cols.at[0:16], east_next, (west, south)),
        (first_cols.at[8:24], east_prev, (west, north)),
        (last_cols.at[0:16], west_next, (east, south)),
        (last_cols.at[8:24], west_prev, (east, north)),
    ]
    copies = [
        pltpu.make_async_remote_copy(
            src_ref=src, dst_ref=dst, send_sem=halo_send.at[i], recv_sem=halo_recv.at[i],
            device_id=target, device_id_type=MESH,
        )
        for i, (src, dst, target) in enumerate(plan)
    ]
    for copy in copies:
        copy.start()

    for copy in copies[2:]:
        copy.wait_recv()
    sub = lax.broadcasted_iota(jnp.int32, (8, LANES), 0)
    lane48 = lax.broadcasted_iota(jnp.int32, (high, LANES), 1)

    def stack(mid, after, before):
        return jnp.concatenate(
            [mid[...], after[0:8], jnp.where(sub < 4, after[8:16], before[0:8]), before[8:16]], axis=0
        )

    east_all = stack(east_mid, east_next, east_prev)
    west_all = stack(west_mid, west_next, west_prev)
    for k in range(total):
        right = pltpu.roll(east_all, (LANES - EDGE * k) % LANES, 1) if k else east_all
        left = pltpu.roll(west_all, (2 * LANES - EDGE - EDGE * k) % LANES, 1)
        ext[k, :, cols:wide] = jnp.where(lane48 < LANES // 2, right, left)
    for copy in copies[:2]:
        copy.wait_recv()
    for k in range(total):
        ext[k, rows : rows + ITERS, 0:cols] = from_next[ITERS * k : ITERS * (k + 1), :]
        ext[k, high - ITERS : high, 0:cols] = from_prev[ITERS * k : ITERS * (k + 1), :]
    row_id = lax.broadcasted_iota(jnp.int32, (high, wide), 0)
    lowest = jnp.where(gy == 0, 36, high)
    highest = jnp.where(gy == ny - 1, rows, 36)
    outside = ((row_id >= highest) & (row_id < 36)) | (row_id >= lowest)
    wet_all = jnp.where(outside, 0.0, ext[total - 1])

    def up(array, axis):
        return pltpu.roll(array, array.shape[axis] - 1, axis)

    wet_east = wet_all * up(wet_all, 1)
    wet_north = wet_all * up(wet_all, 0)
    for level in range(nlevels):
        diffuse = ext[layers + level]
        c_east[level] = 0.5 * (diffuse + up(diffuse, 1)) * wet_east
        c_north[level] = 0.5 * (diffuse + up(diffuse, 0)) * wet_north
    for level in range(nlevels):

        def advance(_, fields):
            ce, cn = c_east[level], c_north[level]
            out = []
            for f in fields:
                flux_e = ce * (up(f, 1) - f)
                flux_n = cn * (up(f, 0) - f)
                f = f + (flux_e - pltpu.roll(flux_e, 1, 1)) + (flux_n - pltpu.roll(flux_n, 1, 0))
                out.append(f)
            return tuple(out)

        fields = lax.fori_loop(
            0, ITERS, advance, tuple(ext[f * nlevels + level] for f in range(nfields))
        )
        for f in range(nfields):
            k = f * nlevels + level
            smoothed[f, level] = fields[f][0:rows, 0:cols]
            for half in range(cols // LANES):
                at = (half * layers + k) * rows
                table[at : at + rows, :] = fields[f][0:rows, half * LANES : (half + 1) * LANES]
    for copy in copies:
        copy.wait_send()

    slot = lax.broadcasted_iota(jnp.int32, (8, LANES), 0)

    def look_up(group, carry):
        at = [group * GROUP + i for i in range(GROUP)]
        lanes = [cells[0, o, 2] & (LANES - 1) for o in at]
        wanted = [
            (lax.shift_right_logical(cells[0, o, 2], 7) * layers + cells[0, o, 0]) * rows
            + cells[0, o, 1]
            for o in at
        ]

        def scan(step, found):
            for i in range(8):
                r = step * 8 + i
                line = jnp.broadcast_to(table[pl.ds(r, 1), :], (8, LANES))
                found = tuple(
                    jnp.where(
                        w == r,
                        jnp.take_along_axis(line, l, axis=1, mode="promise_in_bounds"),
                        have,
                    )
                    for w, l, have in zip(wanted, lanes, found)
                )
            return found

        zero = jnp.zeros((8, LANES), jnp.float32)
        found = lax.fori_loop(0, table.shape[0] // 8, scan, (zero,) * GROUP)
        for o, value in zip(at, found):
            keep = slot < counts[0, pl.ds(o, 1), :]
            part[o] = jnp.sum(
                jnp.where(keep, weights[0, o] * value, 0.0), axis=0, keepdims=True
            )
        return carry

    lax.fori_loop(0, devices // GROUP, look_up, 0)

    def send(step, carry):
        other, target = place(step)
        pltpu.make_async_remote_copy(
            src_ref=part.at[other], dst_ref=recv.at[me], send_sem=part_send, recv_sem=part_recv,
            device_id=target, device_id_type=MESH,
        ).start()
        return carry

    lax.fori_loop(1, devices, send, 0)
    recv[me] = part[me]
    others = pl.ds(0, devices - 1)
    pltpu.make_async_copy(part.at[others], part.at[others], part_send).wait()
    pltpu.make_async_copy(recv.at[others], recv.at[others], part_recv).wait()

    span = obs.shape[0]
    high_id = lax.broadcasted_iota(jnp.int32, (span, LANES), 0)
    low_id = lax.broadcasted_iota(jnp.int32, (LANES, LANES), 0)

    def gather_up(group, acc):
        left, right = [], []
        for i in range(GROUP):
            o = group * GROUP + i
            value = recv[o]
            target = owner[0, pl.ds(o, 1), :]
            top = value.astype(jnp.bfloat16).astype(jnp.float32)
            rest = value - top
            mid = rest.astype(jnp.bfloat16).astype(jnp.float32)
            pieces = (top, mid, rest - mid)
            hit = high_id == lax.shift_right_logical(target, 7)
            left.append(
                jnp.concatenate(
                    [jnp.where(hit, p, 0.0).astype(jnp.bfloat16) for p in pieces], axis=0
                )
            )
            right.append(
                jnp.where(low_id == (target & (LANES - 1)), 1.0, 0.0).astype(jnp.bfloat16)
            )
        return acc + lax.dot_general(
            jnp.concatenate(left, axis=1), jnp.concatenate(right, axis=1),
            (((1,), (1,)), ((), ())), preferred_element_type=jnp.float32,
        )

    acc = lax.fori_loop(
        0, devices // GROUP, gather_up, jnp.zeros((3 * span, LANES), jnp.float32)
    )
    obs[...] = acc[0:span] + (acc[span : 2 * span] + acc[2 * span : 3 * span])


def local(nx, ny, *args):
    inc = args[0]
    nfields, nlevels, rows, cols = inc.shape
    layers = nfields * nlevels
    total = layers + nlevels + 1
    high, wide = rows + 24, cols + LANES
    packed = -(-ITERS * total // 8) * 8
    devices = nx * ny
    vmem = pl.BlockSpec(memory_space=pltpu.VMEM)
    f32 = jnp.float32
    shapes = [
        (total, high, wide), (nlevels, high, wide), (nlevels, high, wide),
        (packed, cols), (packed, cols), (rows, LANES), (rows, LANES),
        (packed, cols), (packed, cols),
        (rows, LANES), (16, LANES), (16, LANES), (rows, LANES), (16, LANES), (16, LANES),
        (layers * rows * (cols // LANES), LANES), (devices, 1, LANES), (devices, 1, LANES),
    ]
    smoothed, obs = pl.pallas_call(
        functools.partial(kernel, nx, ny),
        out_shape=(
            jax.ShapeDtypeStruct(inc.shape, f32),
            jax.ShapeDtypeStruct((OBS_DEV // LANES, LANES), f32),
        ),
        in_specs=[vmem] * len(args),
        out_specs=(vmem, vmem),
        scratch_shapes=[pltpu.VMEM(s, f32) for s in shapes]
        + [
            pltpu.SemaphoreType.DMA((8,)), pltpu.SemaphoreType.DMA((8,)),
            pltpu.SemaphoreType.DMA, pltpu.SemaphoreType.DMA,
        ],
        compiler_params=pltpu.CompilerParams(
            collective_id=0, has_side_effects=True, vmem_limit_bytes=32 * 1024 * 1024
        ),
        name="smooth_and_observe",
    )(*args)
    return smoothed, obs.reshape(OBS_DEV)


def solution(mesh):
    return jax.shard_map(
        functools.partial(local, mesh.shape["gx"], mesh.shape["gy"]),
        mesh=mesh,
        in_specs=(
            P(None, None, "gy", "gx"),
            P(None, "gy", "gx"),
            P("gy", "gx"),
            P(("gx", "gy"), None, None, None, None),
            P(("gx", "gy"), None, None, None),
            P(("gx", "gy"), None, None),
            P(("gx", "gy"), None, None),
        ),
        out_specs=(P(None, None, "gy", "gx"), P(("gx", "gy"))),
        check_vma=False,
    )
```

time: 332 us -> 66 us (0.20)
  local copies, waits for them, and re-layouts: 188 us -> 7.13 us
  waiting for transfers between devices: 75.5 us -> 0 us
  Pallas kernels: 0 us -> 57.8 us
  other arithmetic: 32.7 us -> 0 us
  starting transfers between devices: 21.7 us -> 0 us
  blocking collectives: 11.7 us -> 0 us
    gather x1 -> x0, local copies, waits for them, and re-layouts: 181 us -> none  [local(): values = flat_tile[flat_index]]
    ppermute x22 -> x0, waiting for transfers between devices: 63.8 us -> none  [the longest x11 54.8 us: padded(): before = lax.ppermute(last, axis, up)]
    pallas_call x0 -> x1, Pallas kernels: none -> 57.8 us  [local(): pl.pallas_call(functools.partial(kernel, nx, ny), out_shape=(jax.ShapeDty...]
    scatter-add x1 -> x0, other arithmetic: 22.5 us -> none  [local(): jnp.zeros((OBS_DEV,), jnp.float32).at[slot_owner[0].reshape(-1)]]
    ppermute x22 -> x0, starting transfers between devices: 15.7 us -> none  [the longest x11 11.2 us: padded(): after = lax.ppermute(first, axis, down)]
    all_to_all x2 -> x0, waiting for transfers between devices: 11.7 us -> none  [the longest x1 6.18 us: local(): lax.all_to_all(partial_value, ('gx', 'gy'), split_axis=0, concat_axis=0,...]
    all_to_all x1 -> x0, blocking collectives: 11.7 us -> none  [local(): lax.all_to_all(stacked, 'gy', split_axis=2, concat_axis=1, tiled=True)]
    all_to_all x2 -> x0, starting transfers between devices: 5.92 us -> none  [the longest x1 3.38 us: local(): lax.all_to_all(jnp.transpose(field, (0, 2, 1)), 'gy', split_axis=1, conca...]
  transfers between devices with their start and end apart: 24 -> 0, of which waited for: 23 -> 0; matrix products, arithmetic and copies ran while one was open for 0% -> 0% of each run, Pallas kernels for 0% -> 0%
where the time goes in v1:
time: 66 us; the launch traced here: 65.6 us
  Pallas kernels  57.8 us (88%)
  local copies, waits for them, and re-layouts  7.13 us (11%)
  between operations  0.66 us (1%)
    pallas_call x1, Pallas kernels, local(): pl.pallas_call(functools.partial(kernel, nx, ny), out_shape=(jax.ShapeDty...  57.8 us
    unnamed x16, local copies, waits for them, and re-layouts  7.13 us

profile of v1, /device:TPU:0, one launch (start us, length us, event | category | flops | bytes accessed | tf_op | source)
XLA Modules:
  0.0 65.6 jit_solution(2849973485216976392)
XLA Ops:
  0.6 0.0 copy-start
  0.6 1.0 %copy-done = s32[1,32,3,8,128]{4,3,2,1,0:T(8,128)S(1)} copy-done((s32[1,32,3,8,128]{4,3,2,1,0:T(8,128)S(1)}, s32[1,32,3,8,128]{4,3,2,1,0:T(8,128)}, u32[]{:S(2)}) %copy-start) | copy-done | bytes 393240
  1.6 0.0 copy-start.1
  1.6 0.9 %copy-done.1 = f32[2,3,24,256]{3,2,1,0:T(8,128)S(1)} copy-done((f32[2,3,24,256]{3,2,1,0:T(8,128)S(1)}, f32[2,3,24,256]{3,2,1,0:T(8,128)}, u32[]{:S(2)}) %copy-start.1) | copy-done | bytes 147480
  2.5 0.0 copy-start.2
  2.5 0.9 %copy-done.2 = f32[1,32,8,128]{3,2,1,0:T(8,128)S(1)} copy-done((f32[1,32,8,128]{3,2,1,0:T(8,128)S(1)}, f32[1,32,8,128]{3,2,1,0:T(8,128)}, u32[]{:S(2)}) %copy-start.2) | copy-done | bytes 131096
  3.4 0.0 copy-start.3
  3.4 0.9 %copy-done.3 = f32[3,24,256]{2,1,0:T(8,128)S(1)} copy-done((f32[3,24,256]{2,1,0:T(8,128)S(1)}, f32[3,24,256]{2,1,0:T(8,128)}, u32[]{:S(2)}) %copy-start.3) | copy-done | bytes 73752
  4.3 0.0 copy-start.4
  4.3 0.7 %copy-done.4 = s32[24,256]{1,0:T(8,128)S(1)} copy-done((s32[24,256]{1,0:T(8,128)S(1)}, s32[24,256]{1,0:T(8,128)}, u32[]{:S(2)}) %copy-start.4) | copy-done | bytes 24600
  5.1 0.0 copy-start.5
  5.1 0.7 %copy-done.5 = s32[1,32,128]{2,1,0:T(8,128)S(1)} copy-done((s32[1,32,128]{2,1,0:T(8,128)S(1)}, s32[1,32,128]{2,1,0:T(8,128)}, u32[]{:S(2)}) %copy-start.5) | copy-done | bytes 16408
  5.8 0.0 copy-start.6
  5.8 0.7 %copy-done.6 = s32[1,32,128]{2,1,0:T(8,128)S(1)} copy-done((s32[1,32,128]{2,1,0:T(8,128)S(1)}, s32[1,32,128]{2,1,0:T(8,128)}, u32[]{:S(2)}) %copy-start.6) | copy-done | bytes 16408
  6.5 57.8 %smooth_and_observe.1 = (f32[2,3,24,256]{3,2,1,0:T(8,128)S(1)}, f32[32,128]{1,0:T(8,128)S(1)}) custom-call(f32[2,3,24,256]{3,2,1,0:T(8,128)S(1)} %copy-done.1, f32[3,24,256]{2,1,0:T(8,128)S(1)} %copy-done.3, s32[24,256]{1,0:T(8,128)S(1)} %copy-done.4, s32[1,32,3,8,128]{4,3,2,1,0:T(8,128)S(1)} %copy-done, f32[1,32,8,128]{3,2,1,0:T(8,128)S(1)} %copy-done.2, ...), custom_call_target="tpu_custom_call" | custom-call | tf_op jit(solution)/shard_map/smooth_and_observe/pallas_call | solution.py:255
  64.3 0.7 %copy.11 = f32[2,3,24,256]{3,2,1,0:T(8,128)} copy(f32[2,3,24,256]{3,2,1,0:T(8,128)S(1)} %get-tuple-element.8) | data formatting | bytes 294912
  65.0 0.6 copy.12
Async XLA Ops:
  0.6 1.0 %copy-start = (s32[1,32,3,8,128]{4,3,2,1,0:T(8,128)S(1)}, s32[1,32,3,8,128]{4,3,2,1,0:T(8,128)}, u32[]{:S(2)}) copy-start(s32[1,32,3,8,128]{4,3,2,1,0:T(8,128)} %cells.1) | copy-start | bytes 1179652
  1.6 0.9 %copy-start.1 = (f32[2,3,24,256]{3,2,1,0:T(8,128)S(1)}, f32[2,3,24,256]{3,2,1,0:T(8,128)}, u32[]{:S(2)}) copy-start(f32[2,3,24,256]{3,2,1,0:T(8,128)} %inc.1) | copy-start | bytes 442372
  2.5 0.9 %copy-start.2 = (f32[1,32,8,128]{3,2,1,0:T(8,128)S(1)}, f32[1,32,8,128]{3,2,1,0:T(8,128)}, u32[]{:S(2)}) copy-start(f32[1,32,8,128]{3,2,1,0:T(8,128)} %weights.1) | copy-start | bytes 393220
  3.4 0.9 %copy-start.3 = (f32[3,24,256]{2,1,0:T(8,128)S(1)}, f32[3,24,256]{2,1,0:T(8,128)}, u32[]{:S(2)}) copy-start(f32[3,24,256]{2,1,0:T(8,128)} %dif.1) | copy-start | bytes 221188
  4.3 0.7 %copy-start.4 = (s32[24,256]{1,0:T(8,128)S(1)}, s32[24,256]{1,0:T(8,128)}, u32[]{:S(2)}) copy-start(s32[24,256]{1,0:T(8,128)} %mask.1) | copy-start | bytes 73732
  5.1 0.7 %copy-start.5 = (s32[1,32,128]{2,1,0:T(8,128)S(1)}, s32[1,32,128]{2,1,0:T(8,128)}, u32[]{:S(2)}) copy-start(s32[1,32,128]{2,1,0:T(8,128)} %counts.1) | copy-start | bytes 49156
  5.8 0.7 %copy-start.6 = (s32[1,32,128]{2,1,0:T(8,128)S(1)}, s32[1,32,128]{2,1,0:T(8,128)}, u32[]{:S(2)}) copy-start(s32[1,32,128]{2,1,0:T(8,128)} %owner.1) | copy-start | bytes 49156

commit v2 on v1

--- a/solution.py
+++ b/solution.py
@@ -16,11 +16,21 @@
 
 
 def kernel(
-    nx, ny, inc, dif, mask, cells, weights, counts, owner, smoothed, obs,
-    ext, c_east, c_north, to_prev, to_next, first_cols, last_cols,
-    from_prev, from_next, east_mid, east_next, east_prev, west_mid, west_next, west_prev,
-    table, part, recv, halo_send, halo_recv, part_send, part_recv,
+    nx, ny, *refs
 ):
+    inputs, (smoothed, obs), held = refs[:7], refs[7:9], refs[9:16]
+    inc, dif, mask, cells, weights, counts, owner = held
+    (
+        ext, c_east, c_north, to_prev, to_next, first_cols, last_cols,
+        from_prev, from_next, east_mid, east_next, east_prev, west_mid, west_next, west_prev,
+        table, pieces, part, recv, load_sem, halo_send, halo_recv, part_send, part_recv,
+    ) = refs[16:]
+    loads = [
+        pltpu.make_async_copy(src, dst, load_sem.at[i])
+        for i, (src, dst) in enumerate(zip(inputs, held))
+    ]
+    for load in loads:
+        load.start()
     nfields, nlevels, rows, cols = inc.shape
     layers = nfields * nlevels
     total = layers + nlevels + 1
@@ -41,6 +51,8 @@
 
     lax.fori_loop(1, devices, greet, 0)
 
+    for load in loads[:3]:
+        load.wait()
     lane = lax.broadcasted_iota(jnp.int32, (rows, LANES), 1)
     wet = mask[...].astype(jnp.float32)
     packed_first = jnp.zeros((rows, LANES), jnp.float32)
@@ -145,47 +157,56 @@
         for f in range(nfields):
             k = f * nlevels + level
             smoothed[f, level] = fields[f][0:rows, 0:cols]
-            for half in range(cols // LANES):
-                at = (half * layers + k) * rows
-                table[at : at + rows, :] = fields[f][0:rows, half * LANES : (half + 1) * LANES]
+            table[k * rows : (k + 1) * rows, :] = fields[f][0:rows, 0:cols]
     for copy in copies:
         copy.wait_send()
-
+    for load in loads[3:]:
+        load.wait()
+
+    lines = table.shape[0]
+    whole = table[...]
+    top = whole.astype(jnp.bfloat16)
+    pieces[0:lines] = top
+    pieces[lines : 2 * lines] = (whole - top.astype(jnp.float32)).astype(jnp.bfloat16)
     slot = lax.broadcasted_iota(jnp.int32, (8, LANES), 0)
-
-    def look_up(group, carry):
-        at = [group * GROUP + i for i in range(GROUP)]
-        lanes = [cells[0, o, 2] & (LANES - 1) for o in at]
-        wanted = [
-            (lax.shift_right_logical(cells[0, o, 2], 7) * layers + cells[0, o, 0]) * rows
-            + cells[0, o, 1]
-            for o in at
-        ]
-
-        def scan(step, found):
-            for i in range(8):
-                r = step * 8 + i
-                line = jnp.broadcast_to(table[pl.ds(r, 1), :], (8, LANES))
-                found = tuple(
-                    jnp.where(
-                        w == r,
-                        jnp.take_along_axis(line, l, axis=1, mode="promise_in_bounds"),
-                        have,
-                    )
-                    for w, l, have in zip(wanted, lanes, found)
+    low16 = lax.broadcasted_iota(jnp.int32, (16, LANES), 0)
+    steps = [(low16 + c).astype(jnp.float32).astype(jnp.bfloat16) for c in range(0, cols, 16)]
+    one, none = jnp.ones((16, LANES), jnp.bfloat16), jnp.zeros((16, LANES), jnp.bfloat16)
+
+    def look_up(o, carry):
+        col = cells[0, o, 2]
+        line = cells[0, o, 0] * rows + cells[0, o, 1]
+        weight = jnp.where(slot < counts[0, pl.ds(o, 1), :], weights[0, o], 0.0)
+        acc = jnp.zeros((8, LANES), jnp.float32)
+        for k in range(0, 8, 2):
+            hot = []
+            for j in (k, k + 1):
+                want = jnp.broadcast_to(col[j : j + 1], (16, LANES))
+                want = want.astype(jnp.float32).astype(jnp.bfloat16)
+                hot.append(
+                    jnp.concatenate([jnp.where(s == want, one, none) for s in steps], axis=0)
                 )
-            return found
-
-        zero = jnp.zeros((8, LANES), jnp.float32)
-        found = lax.fori_loop(0, table.shape[0] // 8, scan, (zero,) * GROUP)
-        for o, value in zip(at, found):
-            keep = slot < counts[0, pl.ds(o, 1), :]
-            part[o] = jnp.sum(
-                jnp.where(keep, weights[0, o] * value, 0.0), axis=0, keepdims=True
+            found = jnp.dot(
+                pieces[...], jnp.concatenate(hot, axis=1), preferred_element_type=jnp.float32
             )
+            found = found[0:lines] + found[lines : 2 * lines]
+            for i, j in enumerate((k, k + 1)):
+                want = jnp.broadcast_to(line[j : j + 1], (8, LANES))
+                tiles = [found[t : t + 8, i * LANES : (i + 1) * LANES] for t in range(0, lines, 8)]
+                bit = 8
+                while len(tiles) > 1:
+                    odd = (want & bit) != 0
+                    tiles = [
+                        jnp.where(odd, tiles[t + 1], tiles[t]) if t + 1 < len(tiles) else tiles[t]
+                        for t in range(0, len(tiles), 2)
+                    ]
+                    bit *= 2
+                scale = jnp.broadcast_to(weight[j : j + 1], (8, LANES))
+                acc = acc + jnp.where(slot == (want & 7), tiles[0], 0.0) * scale
+        part[o] = jnp.sum(acc, axis=0, keepdims=True)
         return carry
 
-    lax.fori_loop(0, devices // GROUP, look_up, 0)
+    lax.fori_loop(0, devices, look_up, 0)
 
     def send(step, carry):
         other, target = place(step)
@@ -214,11 +235,11 @@
             top = value.astype(jnp.bfloat16).astype(jnp.float32)
             rest = value - top
             mid = rest.astype(jnp.bfloat16).astype(jnp.float32)
-            pieces = (top, mid, rest - mid)
+            parts = (top, mid, rest - mid)
             hit = high_id == lax.shift_right_logical(target, 7)
             left.append(
                 jnp.concatenate(
-                    [jnp.where(hit, p, 0.0).astype(jnp.bfloat16) for p in pieces], axis=0
+                    [jnp.where(hit, p, 0.0).astype(jnp.bfloat16) for p in parts], axis=0
                 )
             )
             right.append(
@@ -250,23 +271,27 @@
         (packed, cols), (packed, cols), (rows, LANES), (rows, LANES),
         (packed, cols), (packed, cols),
         (rows, LANES), (16, LANES), (16, LANES), (rows, LANES), (16, LANES), (16, LANES),
-        (layers * rows * (cols // LANES), LANES), (devices, 1, LANES), (devices, 1, LANES),
+        (layers * rows, cols),
     ]
+    slots = pltpu.VMEM((devices, 1, LANES), f32)
     smoothed, obs = pl.pallas_call(
         functools.partial(kernel, nx, ny),
         out_shape=(
             jax.ShapeDtypeStruct(inc.shape, f32),
             jax.ShapeDtypeStruct((OBS_DEV // LANES, LANES), f32),
         ),
-        in_specs=[vmem] * len(args),
+        in_specs=[pl.BlockSpec(memory_space=pl.ANY)] * len(args),
         out_specs=(vmem, vmem),
-        scratch_shapes=[pltpu.VMEM(s, f32) for s in shapes]
+        scratch_shapes=[pltpu.VMEM(a.shape, a.dtype) for a in args]
+        + [pltpu.VMEM(s, f32) for s in shapes]
+        + [pltpu.VMEM((2 * layers * rows, cols), jnp.bfloat16), slots, slots]
         + [
+            pltpu.SemaphoreType.DMA((len(args),)),
             pltpu.SemaphoreType.DMA((8,)), pltpu.SemaphoreType.DMA((8,)),
             pltpu.SemaphoreType.DMA, pltpu.SemaphoreType.DMA,
         ],
         compiler_params=pltpu.CompilerParams(
-            collective_id=0, has_side_effects=True, vmem_limit_bytes=32 * 1024 * 1024
+            collective_id=0, has_side_effects=True, vmem_limit_bytes=56 * 1024 * 1024
         ),
         name="smooth_and_observe",
     )(*args)

time: 66 us -> 36.9 us (0.56)
  Pallas kernels: 57.8 us -> 33.9 us
  local copies, waits for them, and re-layouts: 7.13 us -> 2.2 us
    pallas_call x1, Pallas kernels: 57.8 us -> 33.9 us  [local(): pl.pallas_call(functools.partial(kernel, nx, ny), out_shape=(jax.ShapeDty...]
    unnamed x16 -> x4, local copies, waits for them, and re-layouts: 7.13 us -> 2.2 us
where the time goes in v2:
time: 36.9 us; the launch traced here: 36.7 us
  Pallas kernels  33.9 us (92%)
  local copies, waits for them, and re-layouts  2.2 us (6%)
  between operations  0.65 us (2%)
    pallas_call x1, Pallas kernels, local(): pl.pallas_call(functools.partial(kernel, nx, ny), out_shape=(jax.ShapeDty...  33.9 us
    unnamed x4, local copies, waits for them, and re-layouts  2.2 us

profile of v2, /device:TPU:0, one launch (start us, length us, event | category | flops | bytes accessed | tf_op | source)
XLA Modules:
  0.0 36.7 jit_solution(5430434925028075449)
XLA Ops:
  0.6 33.9 %smooth_and_observe.1 = (f32[2,3,24,256]{3,2,1,0:T(8,128)}, f32[32,128]{1,0:T(8,128)}) custom-call(f32[2,3,24,256]{3,2,1,0:T(8,128)} %refs_0_.1, f32[3,24,256]{2,1,0:T(8,128)} %refs_1_.1, s32[24,256]{1,0:T(8,128)} %refs_2_.1, s32[1,32,3,8,128]{4,3,2,1,0:T(8,128)} %refs_3_.1, f32[1,32,8,128]{3,2,1,0:T(8,128)} %refs_4_.1, s32[1,32,128]{2,1,0:T(8,128)} %refs_5_.1, ...), custom_call_target="tpu_custom_call" | custom-call | tf_op jit(solution)/shard_map/smooth_and_observe/pallas_call | solution.py:277
  34.5 0.0 copy-start
  34.5 1.6 %copy.11 = f32[2,3,24,256]{3,2,1,0:T(8,128)} copy(f32[2,3,24,256]{3,2,1,0:T(8,128)} %get-tuple-element.8) | data formatting | bytes 294912
  36.1 0.0 copy-done
  36.1 0.6 %copy.12 = f32[4096]{0:T(1024)} copy(f32[4096]{0:T(1024)S(1)} %bitcast.1) | data formatting | bytes 32768
Async XLA Ops:
  34.5 1.6 %copy-start = (f32[32,128]{1,0:T(8,128)S(1)}, f32[32,128]{1,0:T(8,128)}, u32[]{:S(2)}) copy-start(f32[32,128]{1,0:T(8,128)} %get-tuple-element.5) | copy-start | bytes 49156

commit v3 on v2

--- a/solution.py
+++ b/solution.py
@@ -11,6 +11,7 @@
 OBS_DEV = 4096
 LANES = 128
 EDGE = 12
+TOGETHER = 4
 MESH = pl.DeviceIdType.MESH
 GROUP = 8
 
@@ -173,7 +174,7 @@
     steps = [(low16 + c).astype(jnp.float32).astype(jnp.bfloat16) for c in range(0, cols, 16)]
     one, none = jnp.ones((16, LANES), jnp.bfloat16), jnp.zeros((16, LANES), jnp.bfloat16)
 
-    def look_up(o, carry):
+    def look_up(o):
         col = cells[0, o, 2]
         line = cells[0, o, 0] * rows + cells[0, o, 1]
         weight = jnp.where(slot < counts[0, pl.ds(o, 1), :], weights[0, o], 0.0)
@@ -204,19 +205,27 @@
                 scale = jnp.broadcast_to(weight[j : j + 1], (8, LANES))
                 acc = acc + jnp.where(slot == (want & 7), tiles[0], 0.0) * scale
         part[o] = jnp.sum(acc, axis=0, keepdims=True)
-        return carry
-
-    lax.fori_loop(0, devices, look_up, 0)
-
-    def send(step, carry):
-        other, target = place(step)
+
+    def send(other, target):
         pltpu.make_async_remote_copy(
             src_ref=part.at[other], dst_ref=recv.at[me], send_sem=part_send, recv_sem=part_recv,
             device_id=target, device_id_type=MESH,
         ).start()
+
+    def several(group, carry):
+        at = [place(group * TOGETHER + i) for i in range(TOGETHER)]
+        for o, _ in at:
+            look_up(o)
+        for o, target in at:
+            send(o, target)
         return carry
 
-    lax.fori_loop(1, devices, send, 0)
+    lax.fori_loop(1, devices // TOGETHER, several, 0)
+    at = [place(i) for i in range(TOGETHER)]
+    for o, _ in at:
+        look_up(o)
+    for o, target in at[1:]:
+        send(o, target)
     recv[me] = part[me]
     others = pl.ds(0, devices - 1)
     pltpu.make_async_copy(part.at[others], part.at[others], part_send).wait()
@@ -280,7 +289,7 @@
             jax.ShapeDtypeStruct(inc.shape, f32),
             jax.ShapeDtypeStruct((OBS_DEV // LANES, LANES), f32),
         ),
-        in_specs=[pl.BlockSpec(memory_space=pl.ANY)] * len(args),
+        in_specs=[pl.BlockSpec(memory_space=pltpu.HBM)] * len(args),
         out_specs=(vmem, vmem),
         scratch_shapes=[pltpu.VMEM(a.shape, a.dtype) for a in args]
         + [pltpu.VMEM(s, f32) for s in shapes]

time: 36.9 us -> 32.6 us (0.88)
  Pallas kernels: 33.9 us -> 29.6 us
    pallas_call x1, Pallas kernels: 33.9 us -> 29.6 us  [local(): pl.pallas_call(functools.partial(kernel, nx, ny), out_shape=(jax.ShapeDty...]
where the time goes in v3:
time: 32.6 us; the launch traced here: 32.4 us
  Pallas kernels  29.6 us (91%)
  local copies, waits for them, and re-layouts  2.2 us (7%)
  between operations  0.65 us (2%)
    pallas_call x1, Pallas kernels, local(): pl.pallas_call(functools.partial(kernel, nx, ny), out_shape=(jax.ShapeDty...  29.6 us
    unnamed x4, local copies, waits for them, and re-layouts  2.2 us

profile of v3, /device:TPU:0, one launch (start us, length us, event | category | flops | bytes accessed | tf_op | source)
XLA Modules:
  0.0 32.4 jit_solution(10620814013836071448)
XLA Ops:
  0.6 29.6 %smooth_and_observe.1 = (f32[2,3,24,256]{3,2,1,0:T(8,128)}, f32[32,128]{1,0:T(8,128)}) custom-call(f32[2,3,24,256]{3,2,1,0:T(8,128)} %refs_0_.1, f32[3,24,256]{2,1,0:T(8,128)} %refs_1_.1, s32[24,256]{1,0:T(8,128)} %refs_2_.1, s32[1,32,3,8,128]{4,3,2,1,0:T(8,128)} %refs_3_.1, f32[1,32,8,128]{3,2,1,0:T(8,128)} %refs_4_.1, s32[1,32,128]{2,1,0:T(8,128)} %refs_5_.1, ...), custom_call_target="tpu_custom_call" | custom-call | tf_op jit(solution)/shard_map/smooth_and_observe/pallas_call | solution.py:286
  30.2 0.0 copy-start
  30.2 1.6 %copy.11 = f32[2,3,24,256]{3,2,1,0:T(8,128)} copy(f32[2,3,24,256]{3,2,1,0:T(8,128)} %get-tuple-element.8) | data formatting | bytes 294912
  31.8 0.0 copy-done
  31.8 0.6 %copy.12 = f32[4096]{0:T(1024)} copy(f32[4096]{0:T(1024)S(1)} %bitcast.1) | data formatting | bytes 32768
Async XLA Ops:
  30.2 1.6 %copy-start = (f32[32,128]{1,0:T(8,128)S(1)}, f32[32,128]{1,0:T(8,128)}, u32[]{:S(2)}) copy-start(f32[32,128]{1,0:T(8,128)} %get-tuple-element.5) | copy-start | bytes 49156

commit v4 on v3

--- a/solution.py
+++ b/solution.py
@@ -140,42 +140,46 @@
         diffuse = ext[layers + level]
         c_east[level] = 0.5 * (diffuse + up(diffuse, 1)) * wet_east
         c_north[level] = 0.5 * (diffuse + up(diffuse, 0)) * wet_north
-    for level in range(nlevels):
-
-        def advance(_, fields):
-            ce, cn = c_east[level], c_north[level]
-            out = []
-            for f in fields:
-                flux_e = ce * (up(f, 1) - f)
-                flux_n = cn * (up(f, 0) - f)
-                f = f + (flux_e - pltpu.roll(flux_e, 1, 1)) + (flux_n - pltpu.roll(flux_n, 1, 0))
-                out.append(f)
-            return tuple(out)
-
-        fields = lax.fori_loop(
-            0, ITERS, advance, tuple(ext[f * nlevels + level] for f in range(nfields))
-        )
-        for f in range(nfields):
-            k = f * nlevels + level
-            smoothed[f, level] = fields[f][0:rows, 0:cols]
-            table[k * rows : (k + 1) * rows, :] = fields[f][0:rows, 0:cols]
+
+    def advance(_, carry):
+        after = []
+        for k in range(layers):
+            f, ce, cn = ext[k], c_east[k % nlevels], c_north[k % nlevels]
+            flux_e = ce * (up(f, 1) - f)
+            flux_n = cn * (up(f, 0) - f)
+            after.append(
+                f + (flux_e - pltpu.roll(flux_e, 1, 1)) + (flux_n - pltpu.roll(flux_n, 1, 0))
+            )
+        for k in range(layers):
+            ext[k] = after[k]
+        return carry
+
+    lax.fori_loop(0, ITERS, advance, 0)
+    for k in range(layers):
+        table[k // nlevels, k % nlevels] = ext[k, 0:rows, 0:cols]
+    write = pltpu.make_async_copy(table, smoothed, load_sem.at[len(loads)])
+    write.start()
     for copy in copies:
         copy.wait_send()
     for load in loads[3:]:
         load.wait()
 
-    lines = table.shape[0]
-    whole = table[...]
+    lines = layers * rows
+    whole = table[...].reshape(lines, cols)
     top = whole.astype(jnp.bfloat16)
-    pieces[0:lines] = top
-    pieces[lines : 2 * lines] = (whole - top.astype(jnp.float32)).astype(jnp.bfloat16)
+    rest = (whole - top.astype(jnp.float32)).astype(jnp.bfloat16)
+    halves = cols // LANES
+    for h in range(halves):
+        pieces[h * lines : (h + 1) * lines, 0:LANES] = top[:, h * LANES : (h + 1) * LANES]
+        pieces[h * lines : (h + 1) * lines, LANES:] = rest[:, h * LANES : (h + 1) * LANES]
     slot = lax.broadcasted_iota(jnp.int32, (8, LANES), 0)
     low16 = lax.broadcasted_iota(jnp.int32, (16, LANES), 0)
-    steps = [(low16 + c).astype(jnp.float32).astype(jnp.bfloat16) for c in range(0, cols, 16)]
+    steps = [(low16 + c).astype(jnp.float32).astype(jnp.bfloat16) for c in range(0, LANES, 16)]
     one, none = jnp.ones((16, LANES), jnp.bfloat16), jnp.zeros((16, LANES), jnp.bfloat16)
 
     def look_up(o):
-        col = cells[0, o, 2]
+        col = cells[0, o, 2] & (LANES - 1)
+        half = lax.shift_right_logical(cells[0, o, 2], 7)
         line = cells[0, o, 0] * rows + cells[0, o, 1]
         weight = jnp.where(slot < counts[0, pl.ds(o, 1), :], weights[0, o], 0.0)
         acc = jnp.zeros((8, LANES), jnp.float32)
@@ -184,26 +188,34 @@
             for j in (k, k + 1):
                 want = jnp.broadcast_to(col[j : j + 1], (16, LANES))
                 want = want.astype(jnp.float32).astype(jnp.bfloat16)
-                hot.append(
-                    jnp.concatenate([jnp.where(s == want, one, none) for s in steps], axis=0)
-                )
+                one_hot = [jnp.where(s == want, one, none) for s in steps]
+                hot.append(jnp.concatenate(one_hot + one_hot, axis=0))
             found = jnp.dot(
                 pieces[...], jnp.concatenate(hot, axis=1), preferred_element_type=jnp.float32
             )
-            found = found[0:lines] + found[lines : 2 * lines]
             for i, j in enumerate((k, k + 1)):
                 want = jnp.broadcast_to(line[j : j + 1], (8, LANES))
-                tiles = [found[t : t + 8, i * LANES : (i + 1) * LANES] for t in range(0, lines, 8)]
-                bit = 8
-                while len(tiles) > 1:
-                    odd = (want & bit) != 0
+                trees = []
+                for h in range(halves):
                     tiles = [
-                        jnp.where(odd, tiles[t + 1], tiles[t]) if t + 1 < len(tiles) else tiles[t]
-                        for t in range(0, len(tiles), 2)
+                        found[h * lines + t : h * lines + t + 8, i * LANES : (i + 1) * LANES]
+                        for t in range(0, lines, 8)
                     ]
-                    bit *= 2
+                    bit = 8
+                    while len(tiles) > 1:
+                        odd = (want & bit) != 0
+                        tiles = [
+                            jnp.where(odd, tiles[t + 1], tiles[t]) if t + 1 < len(tiles) else tiles[t]
+                            for t in range(0, len(tiles), 2)
+                        ]
+                        bit *= 2
+                    trees += tiles
+                side = jnp.broadcast_to(half[j : j + 1], (8, LANES))
+                picked = trees[0]
+                for h in range(1, halves):
+                    picked = jnp.where(side == h, trees[h], picked)
                 scale = jnp.broadcast_to(weight[j : j + 1], (8, LANES))
-                acc = acc + jnp.where(slot == (want & 7), tiles[0], 0.0) * scale
+                acc = acc + jnp.where(slot == (want & 7), picked, 0.0) * scale
         part[o] = jnp.sum(acc, axis=0, keepdims=True)
 
     def send(other, target):
@@ -262,6 +274,7 @@
     acc = lax.fori_loop(
         0, devices // GROUP, gather_up, jnp.zeros((3 * span, LANES), jnp.float32)
     )
+    write.wait()
     obs[...] = acc[0:span] + (acc[span : 2 * span] + acc[2 * span : 3 * span])
 
 
@@ -280,7 +293,7 @@
         (packed, cols), (packed, cols), (rows, LANES), (rows, LANES),
         (packed, cols), (packed, cols),
         (rows, LANES), (16, LANES), (16, LANES), (rows, LANES), (16, LANES), (16, LANES),
-        (layers * rows, cols),
+        inc.shape,
     ]
     slots = pltpu.VMEM((devices, 1, LANES), f32)
     smoothed, obs = pl.pallas_call(
@@ -290,12 +303,12 @@
             jax.ShapeDtypeStruct((OBS_DEV // LANES, LANES), f32),
         ),
         in_specs=[pl.BlockSpec(memory_space=pltpu.HBM)] * len(args),
-        out_specs=(vmem, vmem),
+        out_specs=(pl.BlockSpec(memory_space=pltpu.HBM), vmem),
         scratch_shapes=[pltpu.VMEM(a.shape, a.dtype) for a in args]
         + [pltpu.VMEM(s, f32) for s in shapes]
-        + [pltpu.VMEM((2 * layers * rows, cols), jnp.bfloat16), slots, slots]
+        + [pltpu.VMEM((layers * rows * (cols // LANES), 2 * LANES), jnp.bfloat16), slots, slots]
         + [
-            pltpu.SemaphoreType.DMA((len(args),)),
+            pltpu.SemaphoreType.DMA((len(args) + 1,)),
             pltpu.SemaphoreType.DMA((8,)), pltpu.SemaphoreType.DMA((8,)),
             pltpu.SemaphoreType.DMA, pltpu.SemaphoreType.DMA,
         ],

time: 32.6 us -> 31.9 us (0.979)
  Pallas kernels: 29.6 us -> 28.9 us
    pallas_call x1, Pallas kernels: 29.6 us -> 28.9 us  [local(): pl.pallas_call(functools.partial(kernel, nx, ny), out_shape=(jax.ShapeDty...]
where the time goes in v4:
time: 31.9 us; the launch traced here: 31.7 us
  Pallas kernels  28.9 us (91%)
  local copies, waits for them, and re-layouts  2.2 us (7%)
  between operations  0.65 us (2%)
    pallas_call x1, Pallas kernels, local(): pl.pallas_call(functools.partial(kernel, nx, ny), out_shape=(jax.ShapeDty...  28.9 us
    unnamed x4, local copies, waits for them, and re-layouts  2.2 us

profile of v4, /device:TPU:0, one launch (start us, length us, event | category | flops | bytes accessed | tf_op | source)
XLA Modules:
  0.0 31.7 jit_solution(9922448440216530868)
XLA Ops:
  0.6 28.9 %smooth_and_observe.1 = (f32[2,3,24,256]{3,2,1,0:T(8,128)}, f32[32,128]{1,0:T(8,128)}) custom-call(f32[2,3,24,256]{3,2,1,0:T(8,128)} %refs_0_.1, f32[3,24,256]{2,1,0:T(8,128)} %refs_1_.1, s32[24,256]{1,0:T(8,128)} %refs_2_.1, s32[1,32,3,8,128]{4,3,2,1,0:T(8,128)} %refs_3_.1, f32[1,32,8,128]{3,2,1,0:T(8,128)} %refs_4_.1, s32[1,32,128]{2,1,0:T(8,128)} %refs_5_.1, ...), custom_call_target="tpu_custom_call" | custom-call | tf_op jit(solution)/shard_map/smooth_and_observe/pallas_call | solution.py:299
  29.5 0.0 copy-start
  29.5 1.6 %copy.11 = f32[2,3,24,256]{3,2,1,0:T(8,128)} copy(f32[2,3,24,256]{3,2,1,0:T(8,128)} %get-tuple-element.8) | data formatting | bytes 294912
  31.1 0.0 copy-done
  31.1 0.6 %copy.12 = f32[4096]{0:T(1024)} copy(f32[4096]{0:T(1024)S(1)} %bitcast.1) | data formatting | bytes 32768
Async XLA Ops:
  29.5 1.6 %copy-start = (f32[32,128]{1,0:T(8,128)S(1)}, f32[32,128]{1,0:T(8,128)}, u32[]{:S(2)}) copy-start(f32[32,128]{1,0:T(8,128)} %get-tuple-element.5) | copy-start | bytes 49156

commit v5 on v4

--- a/solution.py
+++ b/solution.py
@@ -177,46 +177,62 @@
     steps = [(low16 + c).astype(jnp.float32).astype(jnp.bfloat16) for c in range(0, LANES, 16)]
     one, none = jnp.ones((16, LANES), jnp.bfloat16), jnp.zeros((16, LANES), jnp.bfloat16)
 
-    def look_up(o):
-        col = cells[0, o, 2] & (LANES - 1)
-        half = lax.shift_right_logical(cells[0, o, 2], 7)
-        line = cells[0, o, 0] * rows + cells[0, o, 1]
-        weight = jnp.where(slot < counts[0, pl.ds(o, 1), :], weights[0, o], 0.0)
-        acc = jnp.zeros((8, LANES), jnp.float32)
-        for k in range(0, 8, 2):
-            hot = []
-            for j in (k, k + 1):
-                want = jnp.broadcast_to(col[j : j + 1], (16, LANES))
-                want = want.astype(jnp.float32).astype(jnp.bfloat16)
-                one_hot = [jnp.where(s == want, one, none) for s in steps]
-                hot.append(jnp.concatenate(one_hot + one_hot, axis=0))
-            found = jnp.dot(
-                pieces[...], jnp.concatenate(hot, axis=1), preferred_element_type=jnp.float32
-            )
-            for i, j in enumerate((k, k + 1)):
-                want = jnp.broadcast_to(line[j : j + 1], (8, LANES))
-                trees = []
-                for h in range(halves):
+    def product(col, k):
+        hot = []
+        for j in (k, k + 1):
+            want = jnp.broadcast_to(col[j : j + 1], (16, LANES))
+            want = want.astype(jnp.float32).astype(jnp.bfloat16)
+            one_hot = [jnp.where(s == want, one, none) for s in steps]
+            hot.append(jnp.concatenate(one_hot + one_hot, axis=0))
+        return jnp.dot(
+            pieces[...], jnp.concatenate(hot, axis=1), preferred_element_type=jnp.float32
+        )
+
+    def select(found, acc, line, half, weight, k):
+        for i, j in enumerate((k, k + 1)):
+            want = jnp.broadcast_to(line[j : j + 1], (8, LANES))
+            trees = []
+            for h in range(halves):
+                tiles = [
+                    found[h * lines + t : h * lines + t + 8, i * LANES : (i + 1) * LANES]
+                    for t in range(0, lines, 8)
+                ]
+                bit = 8
+                while len(tiles) > 1:
+                    odd = (want & bit) != 0
                     tiles = [
-                        found[h * lines + t : h * lines + t + 8, i * LANES : (i + 1) * LANES]
-                        for t in range(0, lines, 8)
+                        jnp.where(odd, tiles[t + 1], tiles[t]) if t + 1 < len(tiles) else tiles[t]
+                        for t in range(0, len(tiles), 2)
                     ]
-                    bit = 8
-                    while len(tiles) > 1:
-                        odd = (want & bit) != 0
-                        tiles = [
-                            jnp.where(odd, tiles[t + 1], tiles[t]) if t + 1 < len(tiles) else tiles[t]
-                            for t in range(0, len(tiles), 2)
-                        ]
-                        bit *= 2
-                    trees += tiles
-                side = jnp.broadcast_to(half[j : j + 1], (8, LANES))
-                picked = trees[0]
-                for h in range(1, halves):
-                    picked = jnp.where(side == h, trees[h], picked)
-                scale = jnp.broadcast_to(weight[j : j + 1], (8, LANES))
-                acc = acc + jnp.where(slot == (want & 7), picked, 0.0) * scale
-        part[o] = jnp.sum(acc, axis=0, keepdims=True)
+                    bit *= 2
+                trees += tiles
+            side = jnp.broadcast_to(half[j : j + 1], (8, LANES))
+            picked = trees[0]
+            for h in range(1, halves):
+                picked = jnp.where(side == h, trees[h], picked)
+            scale = jnp.broadcast_to(weight[j : j + 1], (8, LANES))
+            acc = acc + jnp.where(slot == (want & 7), picked, 0.0) * scale
+        return acc
+
+    def look_up(owners):
+        waiting = None
+        sums = {}
+        for n, o in enumerate(owners):
+            col = cells[0, o, 2] & (LANES - 1)
+            half = lax.shift_right_logical(cells[0, o, 2], 7)
+            line = cells[0, o, 0] * rows + cells[0, o, 1]
+            weight = jnp.where(slot < counts[0, pl.ds(o, 1), :], weights[0, o], 0.0)
+            sums[n] = jnp.zeros((8, LANES), jnp.float32)
+            for k in range(0, 8, 2):
+                found = product(col, k)
+                if waiting is not None:
+                    m, args = waiting
+                    sums[m] = select(args[0], sums[m], *args[1:])
+                waiting = (n, (found, line, half, weight, k))
+        m, args = waiting
+        sums[m] = select(args[0], sums[m], *args[1:])
+        for n, o in enumerate(owners):
+            part[o] = jnp.sum(sums[n], axis=0, keepdims=True)
 
     def send(other, target):
         pltpu.make_async_remote_copy(
@@ -226,16 +242,14 @@
 
     def several(group, carry):
         at = [place(group * TOGETHER + i) for i in range(TOGETHER)]
-        for o, _ in at:
-            look_up(o)
+        look_up([o for o, _ in at])
         for o, target in at:
             send(o, target)
         return carry
 
     lax.fori_loop(1, devices // TOGETHER, several, 0)
     at = [place(i) for i in range(TOGETHER)]
-    for o, _ in at:
-        look_up(o)
+    look_up([o for o, _ in at])
     for o, target in at[1:]:
         send(o, target)
     recv[me] = part[me]
@@ -272,7 +286,7 @@
         )
 
     acc = lax.fori_loop(
-        0, devices // GROUP, gather_up, jnp.zeros((3 * span, LANES), jnp.float32)
+        0, devices // GROUP, gather_up, jnp.zeros((3 * span, LANES), jnp.float32), unroll=2
     )
     write.wait()
     obs[...] = acc[0:span] + (acc[span : 2 * span] + acc[2 * span : 3 * span])

time: 31.9 us -> 31.5 us (0.987)
  Pallas kernels: 28.9 us -> 28.5 us
where the time goes in v5:
time: 31.5 us; the launch traced here: 31.4 us
  Pallas kernels  28.5 us (90%)
  local copies, waits for them, and re-layouts  2.2 us (7%)
  between operations  0.65 us (2%)
    pallas_call x1, Pallas kernels, local(): pl.pallas_call(functools.partial(kernel, nx, ny), out_shape=(jax.ShapeDty...  28.5 us
    unnamed x4, local copies, waits for them, and re-layouts  2.2 us

profile of v5, /device:TPU:0, one launch (start us, length us, event | category | flops | bytes accessed | tf_op | source)
XLA Modules:
  0.0 31.4 jit_solution(1284150284072397506)
XLA Ops:
  0.6 28.5 %smooth_and_observe.1 = (f32[2,3,24,256]{3,2,1,0:T(8,128)}, f32[32,128]{1,0:T(8,128)}) custom-call(f32[2,3,24,256]{3,2,1,0:T(8,128)} %refs_0_.1, f32[3,24,256]{2,1,0:T(8,128)} %refs_1_.1, s32[24,256]{1,0:T(8,128)} %refs_2_.1, s32[1,32,3,8,128]{4,3,2,1,0:T(8,128)} %refs_3_.1, f32[1,32,8,128]{3,2,1,0:T(8,128)} %refs_4_.1, s32[1,32,128]{2,1,0:T(8,128)} %refs_5_.1, ...), custom_call_target="tpu_custom_call" | custom-call | tf_op jit(solution)/shard_map/smooth_and_observe/pallas_call | solution.py:313
  29.2 0.0 copy-start
  29.2 1.6 %copy.11 = f32[2,3,24,256]{3,2,1,0:T(8,128)} copy(f32[2,3,24,256]{3,2,1,0:T(8,128)} %get-tuple-element.8) | data formatting | bytes 294912
  30.8 0.0 copy-done
  30.8 0.6 %copy.12 = f32[4096]{0:T(1024)} copy(f32[4096]{0:T(1024)S(1)} %bitcast.1) | data formatting | bytes 32768
Async XLA Ops:
  29.2 1.6 %copy-start = (f32[32,128]{1,0:T(8,128)S(1)}, f32[32,128]{1,0:T(8,128)}, u32[]{:S(2)}) copy-start(f32[32,128]{1,0:T(8,128)} %get-tuple-element.5) | copy-start | bytes 49156

commit v6 on v5

--- a/solution.py
+++ b/solution.py
@@ -24,7 +24,7 @@
     (
         ext, c_east, c_north, to_prev, to_next, first_cols, last_cols,
         from_prev, from_next, east_mid, east_next, east_prev, west_mid, west_next, west_prev,
-        table, pieces, part, recv, load_sem, halo_send, halo_recv, part_send, part_recv,
+        table, pieces, low_hot, part, recv, load_sem, halo_send, halo_recv, part_send, part_recv,
     ) = refs[16:]
     loads = [
         pltpu.make_async_copy(src, dst, load_sem.at[i])
@@ -56,8 +56,6 @@
         load.wait()
     lane = lax.broadcasted_iota(jnp.int32, (rows, LANES), 1)
     wet = mask[...].astype(jnp.float32)
-    packed_first = jnp.zeros((rows, LANES), jnp.float32)
-    packed_last = jnp.zeros((rows, LANES), jnp.float32)
     for k in range(total):
         if k < layers:
             value = inc[k // nlevels, k % nlevels] * wet
@@ -69,16 +67,6 @@
         ext[k, 32:40, 0:cols] = jnp.zeros((8, cols), jnp.float32)
         to_next[ITERS * k : ITERS * (k + 1), :] = value[rows - ITERS : rows]
         to_prev[ITERS * k : ITERS * (k + 1), :] = value[0:ITERS]
-        here = (lane >= EDGE * k) & (lane < EDGE * (k + 1))
-        first = value[:, 0:LANES]
-        last = value[:, cols - LANES : cols]
-        if k:
-            first = pltpu.roll(first, EDGE * k, 1)
-        last = pltpu.roll(last, (EDGE * k + EDGE) % LANES, 1)
-        packed_first = jnp.where(here, first, packed_first)
-        packed_last = jnp.where(here, last, packed_last)
-    first_cols[...] = packed_first
-    last_cols[...] = packed_last
 
     pl.semaphore_wait(barrier, devices - 1)
 
@@ -101,8 +89,34 @@
         )
         for i, (src, dst, target) in enumerate(plan)
     ]
-    for copy in copies:
+    for copy in copies[:2]:
         copy.start()
+    packed_first = jnp.zeros((rows, LANES), jnp.float32)
+    packed_last = jnp.zeros((rows, LANES), jnp.float32)
+    for k in range(total):
+        value = ext[k, 0:rows, 0:cols]
+        here = (lane >= EDGE * k) & (lane < EDGE * (k + 1))
+        first = value[:, 0:LANES]
+        last = value[:, cols - LANES : cols]
+        if k:
+            first = pltpu.roll(first, EDGE * k, 1)
+        last = pltpu.roll(last, (EDGE * k + EDGE) % LANES, 1)
+        packed_first = jnp.where(here, first, packed_first)
+        packed_last = jnp.where(here, last, packed_last)
+    first_cols[...] = packed_first
+    last_cols[...] = packed_last
+    for copy in copies[2:]:
+        copy.start()
+
+    loads[6].wait()
+    low_id = lax.broadcasted_iota(jnp.int32, (LANES, LANES), 0)
+
+    def mark(o, carry):
+        low = owner[0, pl.ds(o, 1), :] & (LANES - 1)
+        low_hot[o] = jnp.where(low_id == low, 1.0, 0.0).astype(jnp.bfloat16)
+        return carry
+
+    lax.fori_loop(0, devices, mark, 0, unroll=2)
 
     for copy in copies[2:]:
         copy.wait_recv()
@@ -161,7 +175,7 @@
     write.start()
     for copy in copies:
         copy.wait_send()
-    for load in loads[3:]:
+    for load in loads[3:6]:
         load.wait()
 
     lines = layers * rows
@@ -259,7 +273,6 @@
 
     span = obs.shape[0]
     high_id = lax.broadcasted_iota(jnp.int32, (span, LANES), 0)
-    low_id = lax.broadcasted_iota(jnp.int32, (LANES, LANES), 0)
 
     def gather_up(group, acc):
         left, right = [], []
@@ -277,9 +290,7 @@
                     [jnp.where(hit, p, 0.0).astype(jnp.bfloat16) for p in parts], axis=0
                 )
             )
-            right.append(
-                jnp.where(low_id == (target & (LANES - 1)), 1.0, 0.0).astype(jnp.bfloat16)
-            )
+            right.append(low_hot[o])
         return acc + lax.dot_general(
             jnp.concatenate(left, axis=1), jnp.concatenate(right, axis=1),
             (((1,), (1,)), ((), ())), preferred_element_type=jnp.float32,
@@ -320,7 +331,8 @@
         out_specs=(pl.BlockSpec(memory_space=pltpu.HBM), vmem),
         scratch_shapes=[pltpu.VMEM(a.shape, a.dtype) for a in args]
         + [pltpu.VMEM(s, f32) for s in shapes]
-        + [pltpu.VMEM((layers * rows * (cols // LANES), 2 * LANES), jnp.bfloat16), slots, slots]
+        + [pltpu.VMEM((layers * rows * (cols // LANES), 2 * LANES), jnp.bfloat16)]
+        + [pltpu.VMEM((devices, LANES, LANES), jnp.bfloat16), slots, slots]
         + [
             pltpu.SemaphoreType.DMA((len(args) + 1,)),
             pltpu.SemaphoreType.DMA((8,)), pltpu.SemaphoreType.DMA((8,)),

time: 31.5 us -> 31.7 us (level)
  no operation moved by 1% of the time
where the time goes in v6:
time: 31.7 us; the launch traced here: 31.5 us
  Pallas kernels  28.7 us (91%)
  local copies, waits for them, and re-layouts  2.2 us (7%)
  between operations  0.65 us (2%)
    pallas_call x1, Pallas kernels, local(): pl.pallas_call(functools.partial(kernel, nx, ny), out_shape=(jax.ShapeDty...  28.7 us
    unnamed x4, local copies, waits for them, and re-layouts  2.2 us

profile of v6, /device:TPU:0, one launch (start us, length us, event | category | flops | bytes accessed | tf_op | source)
XLA Modules:
  0.0 31.5 jit_solution(14048773218631348706)
XLA Ops:
  0.6 28.7 %smooth_and_observe.1 = (f32[2,3,24,256]{3,2,1,0:T(8,128)}, f32[32,128]{1,0:T(8,128)}) custom-call(f32[2,3,24,256]{3,2,1,0:T(8,128)} %refs_0_.1, f32[3,24,256]{2,1,0:T(8,128)} %refs_1_.1, s32[24,256]{1,0:T(8,128)} %refs_2_.1, s32[1,32,3,8,128]{4,3,2,1,0:T(8,128)} %refs_3_.1, f32[1,32,8,128]{3,2,1,0:T(8,128)} %refs_4_.1, s32[1,32,128]{2,1,0:T(8,128)} %refs_5_.1, ...), custom_call_target="tpu_custom_call" | custom-call | tf_op jit(solution)/shard_map/smooth_and_observe/pallas_call | solution.py:324
  29.3 0.0 copy-start
  29.3 1.6 %copy.11 = f32[2,3,24,256]{3,2,1,0:T(8,128)} copy(f32[2,3,24,256]{3,2,1,0:T(8,128)} %get-tuple-element.8) | data formatting | bytes 294912
  30.9 0.0 copy-done
  30.9 0.6 %copy.12 = f32[4096]{0:T(1024)} copy(f32[4096]{0:T(1024)S(1)} %bitcast.1) | data formatting | bytes 32768
Async XLA Ops:
  29.3 1.6 %copy-start = (f32[32,128]{1,0:T(8,128)S(1)}, f32[32,128]{1,0:T(8,128)}, u32[]{:S(2)}) copy-start(f32[32,128]{1,0:T(8,128)} %get-tuple-element.5) | copy-start | bytes 49156
